TPU v7x, 256 devices: a whole 4x4x8 slice. The times are simulated.
256 devices in a mesh: fsdp: 16 (over x_lo, z), factor: 16 (over x_hi, y, core).
Axes of the slice: x: 4 (x_hi: 2, x_lo: 2; x = x_hi * 2 + x_lo), y: 4, z: 8, core: 2. Of those that a mesh axis runs over, the one named last changes fastest.
Arguments:
- activations: bfloat16 [256, 16, 16, 512], P(('fsdp', 'factor')), may hold values from -12 to 12
- cotangent: bfloat16 [256, 16, 16, 512], P(('fsdp', 'factor')), may hold values from -0.23632812 to 0.23632812
- weight: bfloat16 [4608, 512], P('fsdp'), may hold values from -0.09375 to 0.09375
- a_factor_old: float32 [4608, 4608], P('factor', 'fsdp'), may hold values from -0.11785113 to 5, as said below
- g_factor_old: float32 [512, 512], P('factor'), may hold values from -0.35355339 to 5, as said below
- a_inverse: float32 [4608, 4608], P('fsdp', 'factor'), may hold values from -0.09375 to 0.09375
- g_inverse: float32 [512, 512], replicated, may hold values from -0.25 to 0.25
Outputs:
- conv_out: bfloat16 [256, 16, 16, 512], P(('fsdp', 'factor'))
- a_factor: float32 [4608, 4608], P('factor', 'fsdp')
- g_factor: float32 [512, 512], P('factor')
- natural_grad: bfloat16 [4608, 512], P('fsdp', 'factor')
Inputs may be any that keep to these rules, and one draw needn't show every extreme that they name: `a_factor_old`: a symmetric matrix. `g_factor_old`: a symmetric matrix.
All inputs are finite; a program needn't handle non-finite values.
Results may differ from a plain program's by a relative error of at most 0.0017.
Values may be sent and summed in bfloat16 or wider, within the bound.
A program may use at most 192 MiB of HBM per device.

v0:
```python
import jax
import jax.numpy as jnp
from jax import lax
from jax.sharding import PartitionSpec as P


def unfold(images):
    side = images.shape[1]
    padded = jnp.pad(images, ((0, 0), (1, 1), (1, 1), (0, 0)))
    tap_list = [
        padded[:, row_off : row_off + side, col_off : col_off + side, :]
        for row_off in range(3)
        for col_off in range(3)
    ]
    return jnp.concatenate(tap_list, axis=3).reshape(-1, 9 * images.shape[3])


def contract(first_op, second_op):
    return lax.dot_general(
        first_op, second_op, (((0,), (0,)), ((), ())), preferred_element_type=jnp.float32
    )


def per_device(activations, cotangent, weight, a_factor_old, g_factor_old, a_inverse, g_inverse):
    channels = activations.shape[3]
    own_patches = unfold(activations)
    own_cot = cotangent.reshape(-1, channels)
    factor_index = lax.axis_index("factor")
    rows_per = a_factor_old.shape[0]
    row_start = factor_index * rows_per
    conv_total = jnp.dot(
        own_patches,
        lax.all_gather(weight, "fsdp", axis=0, tiled=True),
        preferred_element_type=jnp.float32,
    )
    conv_out = conv_total.astype(jnp.bfloat16).reshape(activations.shape)
    patches = unfold(lax.all_gather(activations, "factor", axis=0, tiled=True))
    a_partial = contract(lax.dynamic_slice_in_dim(patches, row_start, rows_per, 1), patches)
    grad_partial = lax.psum_scatter(
        contract(own_patches, own_cot), "factor", scatter_dimension=0, tiled=True
    )
    a_summed = lax.psum_scatter(a_partial, "fsdp", scatter_dimension=1, tiled=True)
    pixel_total = float(
        activations.shape[1]
        * activations.shape[2]
        * lax.axis_size("fsdp")
        * lax.axis_size("factor")
    )
    a_factor = 0.5 * a_factor_old + 0.5 * (a_summed / pixel_total)
    grad_rows = lax.psum(grad_partial, "fsdp")
    g_partial = contract(own_cot, own_cot)
    g_rows_count = g_factor_old.shape[0]
    g_summed = lax.psum(g_partial, ("fsdp", "factor"))
    g_rows = lax.dynamic_slice_in_dim(g_summed, factor_index * g_rows_count, g_rows_count, 0)
    g_factor = 0.5 * g_factor_old + 0.5 * g_rows
    mixed = jnp.dot(
        grad_rows, g_inverse, precision=lax.Precision.HIGHEST, preferred_element_type=jnp.float32
    )
    partial_rows = jnp.dot(
        a_inverse, mixed, precision=lax.Precision.HIGHEST, preferred_element_type=jnp.float32
    )
    summed_rows = lax.psum(partial_rows, "factor")
    tile_width = channels // lax.axis_size("factor")
    result_tile = lax.dynamic_slice_in_dim(summed_rows, factor_index * tile_width, tile_width, 1)
    return (conv_out, a_factor, g_factor, result_tile.astype(jnp.bfloat16))


def solution(mesh):
    return jax.shard_map(
        per_device,
        mesh=mesh,
        in_specs=(
            P(("fsdp", "factor"), None, None, None),
            P(("fsdp", "factor"), None, None, None),
            P("fsdp", None),
            P("factor", "fsdp"),
            P("factor", None),
            P("fsdp", "factor"),
            P(),
        ),
        out_specs=(
            P(("fsdp", "factor"), None, None, None),
            P("factor", "fsdp"),
            P("factor", None),
            P("fsdp", "factor"),
        ),
        check_vma=False,
    )
```

profile of v0, /device:TPU:0, one launch (start us, length us, event | category | flops | bytes accessed | tf_op | source)
XLA Modules:
  0.0 599.1 jit_solution(16298183459508021695)
XLA Ops:
  8.0 0.0 copy-start
  8.0 0.0 all-gather.5.cloned.1.call-start
  8.1 0.7 all-gather.5.cloned.1.call-update
  8.8 0.0 reduce-scatter.5.cloned.1.call-start
  8.8 1.0 fusion.10
  9.8 1.0 fusion.11
  10.8 1.0 fusion.12
  11.8 1.0 fusion.13
  12.8 1.0 constant_dynamic-update-slice_fusion
  13.8 1.0 fusion.14
  14.8 1.0 fusion.15
  15.9 1.0 fusion.16
  16.8 0.1 fusion.17
  16.9 1.4 copy-done.6
  18.3 5.1 convolution_bitcast_fusion
  23.4 0.0 reduce-scatter.5.cloned.1.call-update
  23.4 0.0 all-reduce.6.cloned.1.call-start
  23.4 1.3 convolution_bitcast_fusion.2
  24.8 0.0 all-reduce.6.cloned.1.call-update
  24.8 0.0 all-gather.3.cloned.1.call-start
  24.8 0.7 all-gather.3.cloned.1.call-update
  25.5 0.2 all-reduce.8.cloned.1.call-start
  25.8 47.5 %all-gather.5.cloned.1.call-done = bf16[16,16,16,512]{3,2,1,0:T(8,128)(2,1)} async-done(((bf16[1,16,16,512]{3,2,1,0:T(8,128)(2,1)}), bf16[16,16,16,512]{3,2,1,0:T(8,128)(2,1)}) %all-gather.5.cloned.1.call-update) | async-done | bytes 4194320 | tf_op jit(solution)/shard_map/all_gather | solution.py:37
  73.3 5.6 fusion
  78.9 2.7 fusion.1
  81.6 4.1 fusion.2
  85.6 4.2 fusion.3
  89.9 2.8 constant_dynamic-update-slice_fusion.1
  92.6 4.2 fusion.4
  96.9 4.1 fusion.5
  100.9 2.7 fusion.6
  103.7 4.2 fusion.7
  107.9 82.9 %reduce-scatter.5.cloned.1.call-done = f32[288,512]{1,0:T(8,128)} async-done(((f32[4608,512]{1,0:T(8,128)}), f32[288,512]{1,0:T(8,128)}) %reduce-scatter.5.cloned.1.call-update) | async-done | bytes 589840 | tf_op jit(solution)/shard_map/reduce_scatter | solution.py:39
  190.8 0.0 all-reduce.8.cloned.1.call-update
  190.9 0.0 reduce-scatter.7.cloned.1.call-start
  190.9 27.4 %convolution_bitcast_fusion.1 = f32[4608,288]{1,0:T(8,128)} fusion(bf16[4096,4608]{1,0:T(8,128)(2,1)} %bitcast.27, s32[]{:T(128)S(6)} %select_n.7), kind=kOutput, calls=%fused_computation.9 | convolution fusion | flops 10871635968 | bytes 46202884
  218.3 0.0 reduce-scatter.7.cloned.1.call-update
  218.4 91.2 %all-reduce.6.cloned.1.call-done = f32[512,512]{1,0:T(8,128)} async-done(((f32[512,512]{1,0:T(8,128)}), f32[512,512]{1,0:T(8,128)}) %all-reduce.6.cloned.1.call-update) | async-done | bytes 1048592 | tf_op jit(solution)/shard_map/psum | solution.py:53
  309.5 1.5 add_multiply_fusion
  311.0 5.2 convolution_convert_fusion
  316.2 130.5 %all-reduce.8.cloned.1.call-done = f32[288,512]{1,0:T(8,128)} async-done(((f32[288,512]{1,0:T(8,128)}), f32[288,512]{1,0:T(8,128)}) %all-reduce.8.cloned.1.call-update) | async-done | bytes 589840 | tf_op jit(solution)/shard_map/psum | solution.py:50
  446.8 2.2 fusion.21
  449.0 1.1 convolution_bitcast_fusion.3
  450.1 138.8 %all-reduce.9 = bf16[288,512]{1,0:T(8,128)(2,1)S(1)} all-reduce(f32[288,512]{1,0:T(8,128)S(1)} %convolution_bitcast_fusion.3), channel_id=1, replica_groups=mesh['fsdp'=16,'factor'=16] {'factor'}, use_global_device_ids=true, to_apply=%region_4.5 | all-reduce | flops 147456 | bytes 884736 | tf_op jit(solution)/shard_map/psum | solution.py:62
  589.0 0.1 dynamic-slice_convert_fusion
  589.1 0.7 copy.12
  589.8 1.2 copy.14
  591.0 0.8 multiply_add_fusion
  (16 shorter events, 0.0 us)
Async XLA Ops:
  8.0 438.8 %copy-start = (f32[512,512]{1,0:T(8,128)S(1)}, f32[512,512]{1,0:T(8,128)}, u32[]{:S(2)}) copy-start(f32[512,512]{1,0:T(8,128)} %param.13) | copy-start | bytes 3145732
  8.0 8.8 %copy-start.2 = (bf16[1,16,16,512]{3,2,1,0:T(8,128)(2,1)S(1)}, bf16[1,16,16,512]{3,2,1,0:T(8,128)(2,1)}, u32[]{:S(2)}) copy-start(bf16[1,16,16,512]{3,2,1,0:T(8,128)(2,1)} %param.7) | copy-start | bytes 786436
  8.0 10.3 %copy-start.7 = (bf16[1,16,16,512]{3,2,1,0:T(8,128)(2,1)S(1)}, bf16[1,16,16,512]{3,2,1,0:T(8,128)(2,1)}, u32[]{:S(2)}) copy-start(bf16[1,16,16,512]{3,2,1,0:T(8,128)(2,1)} %param.8) | copy-start | bytes 786436
  8.0 65.3 %all-gather.5.cloned.1.call-start = ((), (), s32[]{:S(2)}) async-start(), calls=%async_computation.3 | async-start | bytes 4456448 | tf_op jit(solution)/shard_map/all_gather | solution.py:37
  8.8 182.1 %reduce-scatter.5.cloned.1.call-start = ((), (), s32[]{:S(2)}) async-start(), calls=%async_computation.5 | async-start | bytes 10027008 | tf_op jit(solution)/shard_map/reduce_scatter | solution.py:39
  16.9 1.4 copy-start.6
  23.4 286.2 %all-reduce.6.cloned.1.call-start = ((), (), s32[]{:S(2)}) async-start(), calls=%async_computation.4 | async-start | bytes 2097152 | tf_op jit(solution)/shard_map/psum | solution.py:53
  24.8 286.2 %all-gather.3.cloned.1.call-start = ((), (), s32[]{:S(2)}) async-start(), calls=%async_computation.2 | async-start | bytes 5013504 | tf_op jit(solution)/shard_map/all_gather | solution.py:33
  25.5 421.2 %all-reduce.8.cloned.1.call-start = ((), (), s32[]{:S(2)}) async-start(), calls=%async_computation.6 | async-start | bytes 1179648 | tf_op jit(solution)/shard_map/psum | solution.py:50
  73.3 5.6 copy-start.1
  190.9 398.9 %reduce-scatter.7.cloned.1.call-start = ((), (), s32[]{:S(2)}) async-start(), calls=%async_computation.7 | async-start | bytes 7520256
  218.3 91.2 %copy-start.5 = (f32[32,512]{1,0:T(8,128)S(1)}, f32[32,512]{1,0:T(8,128)}, u32[]{:S(2)}) copy-start(f32[32,512]{1,0:T(8,128)} %param.11) | copy-start | bytes 196612
  311.0 137.9 %copy-start.3 = (f32[288,288]{1,0:T(8,128)S(1)}, f32[288,288]{1,0:T(8,128)}, u32[]{:S(2)}) copy-start(f32[288,288]{1,0:T(8,128)} %param.12) | copy-start | bytes 995332
  316.2 274.8 %copy-start.4 = (f32[288,288]{1,0:T(8,128)S(1)}, f32[288,288]{1,0:T(8,128)}, u32[]{:S(2)}) copy-start(f32[288,288]{1,0:T(8,128)} %param.10) | copy-start | bytes 995332
Sparse Core Ops, SparseCore 0:
  11.6 61.6 all-gather.4
  77.9 112.8 reduce-scatter.4
  192.8 76.6 all-gather.2
Sparse Core Ops, SparseCore 1:
  30.2 279.3 all-reduce.5
  312.0 134.6 all-reduce.7
  449.4 88.0 reduce-scatter.6
where the time goes:
time: 600 us; the launch traced here: 599 us
  waiting for transfers between devices  354 us (59%)
  blocking collectives  139 us (23%)
  local copies, waits for them, and re-layouts  46 us (8%)
  matrix products  42.4 us (7%)
  between operations  15.6 us (3%)
    psum x1, blocking collectives, per_device(): summed_rows = lax.psum(partial_rows, 'factor')  139 us
    psum x1, waiting for transfers between devices, per_device(): grad_rows = lax.psum(grad_partial, 'fsdp')  131 us
    psum x1, waiting for transfers between devices, per_device(): g_summed = lax.psum(g_partial, ('fsdp', 'factor'))  91.2 us
    reduce_scatter x1, waiting for transfers between devices, per_device(): lax.psum_scatter(contract(own_patches, own_cot), 'factor', scatter_dimens...  82.9 us
    all_gather x1, waiting for transfers between devices, per_device(): patches = unfold(lax.all_gather(activations, 'factor', axis=0, tiled=True))  47.5 us
    unnamed x34, local copies, waits for them, and re-layouts  41.7 us
    unnamed x1, matrix products  27.4 us
  transfers between devices with their start and end apart: 6, of which 4 were waited for; matrix products, arithmetic and copies ran while one was open for 15% of the time, Pallas kernels for 0%

commit v1 on v0

--- a/solution.py
+++ b/solution.py
@@ -34,7 +34,12 @@
         preferred_element_type=jnp.float32,
     )
     conv_out = conv_total.astype(jnp.bfloat16).reshape(activations.shape)
-    patches = unfold(lax.all_gather(activations, "factor", axis=0, tiled=True))
+    patches = unfold(
+        jnp.concatenate(
+            lax.all_to_all(jnp.stack([activations] * lax.axis_size("factor")), "factor", 0, 0),
+            axis=0,
+        )
+    )
     a_partial = contract(lax.dynamic_slice_in_dim(patches, row_start, rows_per, 1), patches)
     grad_partial = lax.psum_scatter(
         contract(own_patches, own_cot), "factor", scatter_dimension=0, tiled=True

time: 600 us -> 567 us (0.945)
  blocking collectives: 139 us -> 70.8 us
  waiting for transfers between devices: 354 us -> 369 us
  local copies, waits for them, and re-layouts: 46 us -> 58.5 us
    reduce_scatter x1, waiting for transfers between devices: 82.9 us -> 0.01 us  [per_device(): lax.psum_scatter(contract(own_patches, own_cot), 'factor', scatter_dimens...]
    psum x1, waiting for transfers between devices: 91.2 us -> 170 us  [per_device(): g_summed = lax.psum(g_partial, ('fsdp', 'factor'))]
    psum x1, blocking collectives: 139 us -> 70.8 us  [per_device(): summed_rows = lax.psum(partial_rows, 'factor')]
    all_to_all x0 -> x1, waiting for transfers between devices: none -> 67 us  [per_device(): lax.all_to_all(jnp.stack([activations] * lax.axis_size('factor')), 'facto...]
    all_gather x1 -> x0, waiting for transfers between devices: 47.5 us -> none  [per_device(): patches = unfold(lax.all_gather(activations, 'factor', axis=0, tiled=True))]
    slice x0 -> x1, local copies, waits for them, and re-layouts: none -> 22.1 us  [unfold(): padded[:, row_off:row_off + side, col_off:col_off + side, :]]
    unnamed x34 -> x42, local copies, waits for them, and re-layouts: 41.7 us -> 31.5 us
  transfers between devices with their start and end apart: 6 -> 6, of which waited for: 4 -> 3; matrix products, arithmetic and copies ran while one was open for 15% -> 16% of each run, Pallas kernels for 0% -> 0%
where the time goes in v1:
time: 567 us; the launch traced here: 566 us
  waiting for transfers between devices  369 us (65%)
  blocking collectives  70.8 us (12%)
  local copies, waits for them, and re-layouts  58.5 us (10%)
  matrix products  43.5 us (8%)
  between operations  15.9 us (3%)
  starting transfers between devices  5.96 us (1%)
    psum x1, waiting for transfers between devices, per_device(): g_summed = lax.psum(g_partial, ('fsdp', 'factor'))  170 us
    psum x1, waiting for transfers between devices, per_device(): grad_rows = lax.psum(grad_partial, 'fsdp')  131 us
    psum x1, blocking collectives, per_device(): summed_rows = lax.psum(partial_rows, 'factor')  70.8 us
    all_to_all x1, waiting for transfers between devices, per_device(): lax.all_to_all(jnp.stack([activations] * lax.axis_size('factor')), 'facto...  67 us
    unnamed x42, local copies, waits for them, and re-layouts  31.5 us
    unnamed x1, matrix products  27.5 us
    slice x1, local copies, waits for them, and re-layouts, unfold(): padded[:, row_off:row_off + side, col_off:col_off + side, :]  22.1 us
  transfers between devices with their start and end apart: 6, of which 3 were waited for; matrix products, arithmetic and copies ran while one was open for 16% of the time, Pallas kernels for 0%

profile of v1, /device:TPU:0, one launch (start us, length us, event | category | flops | bytes accessed | tf_op | source)
XLA Modules:
  0.0 565.5 jit_solution(4504686366913387579)
XLA Ops:
  8.0 0.0 all-reduce.6.cloned.1.call-start
  8.1 2.4 convolution_bitcast_fusion.2
  10.5 0.0 all-reduce.6.cloned.1.call-update
  10.5 0.0 reduce-scatter.5.cloned.1.call-start
  10.6 0.1 fusion.2
  10.7 0.1 fusion.4
  10.8 0.1 fusion.5
  10.9 0.1 fusion.6
  10.9 0.1 fusion.7
  11.0 0.1 fusion.9
  11.1 1.4 copy-done.10
  12.5 5.1 convolution_bitcast_fusion
  17.6 0.0 reduce-scatter.5.cloned.1.call-update
  17.6 2.5 stack.2
  20.1 5.3 all-to-all-start
  25.5 0.0 all-gather.2.cloned.1.call-start
  25.5 0.5 all-gather.2.cloned.1.call-update
  26.1 0.2 reduce-scatter.7.cloned.1.call-start
  26.3 67.0 %all-to-all-done = bf16[16,1,16,16,512]{4,3,2,1,0:T(8,128)(2,1)} async-done(((bf16[16,1,16,16,512]{4,3,2,1,0:T(8,128)(2,1)}), bf16[16,1,16,16,512]{4,3,2,1,0:T(8,128)(2,1)}, u32[]{:S(2)}, u32[]{:S(2)}) %all-to-all-start) | async-done | bytes 4194336 | tf_op jit(solution)/shard_map/all_to_all | solution.py:39
  93.3 22.1 %pad_slice_fusion = (bf16[16,16,16,512]{3,2,1,0:T(8,128)(2,1)S(1)}, bf16[16,16,16,512]{3,2,1,0:T(8,128)(2,1)}, bf16[16,16,16,512]{3,2,1,0:T(8,128)(2,1)}, bf16[1...) fusion(bf16[16,16,16,512]{3,2,1,0:T(8,128)(2,1)} %bitcast.3), kind=kLoop, calls=%fused_computation | loop fusion | bytes 37748736 | tf_op jit(solution)/shard_map/slice | solution.py:11
  115.4 4.7 constant_dynamic-update-slice_fusion.9
  120.1 2.4 constant_dynamic-update-slice_fusion.8
  122.5 1.3 copy-done.5
  123.8 2.4 constant_dynamic-update-slice_fusion.7
  126.3 1.3 copy-done.4
  127.5 2.3 constant_dynamic-update-slice_fusion.6
  129.9 4.7 constant_dynamic-update-slice_fusion.5
  134.6 2.5 constant_dynamic-update-slice_fusion.4
  137.0 1.3 copy-done.2
  138.4 2.4 constant_dynamic-update-slice_fusion.3
  140.7 2.4 constant_dynamic-update-slice_fusion.2
  143.1 2.3 constant_dynamic-update-slice_fusion.1
  145.4 27.5 %convolution_bitcast_fusion.1 = f32[4608,288]{1,0:T(8,128)} fusion(bf16[4096,4608]{1,0:T(8,128)(2,1)} %constant_dynamic-update-slice_fusion.1, s32[]{:T(128)S(6)} %select_n.7), kind=kOutput, calls=%fused_computation.9 | convolution fusion | flops 10871635968 | bytes 46202884
  172.9 0.0 reduce-scatter.7.cloned.1.call-update
  172.9 0.3 all-reduce.8.cloned.1.call-start
  173.2 170.0 %all-reduce.6.cloned.1.call-done = f32[512,512]{1,0:T(8,128)} async-done(((f32[512,512]{1,0:T(8,128)}), f32[512,512]{1,0:T(8,128)}) %all-reduce.6.cloned.1.call-update) | async-done | bytes 1048592 | tf_op jit(solution)/shard_map/psum | solution.py:58
  343.2 1.5 add_multiply_fusion
  344.7 0.0 all-reduce.8.cloned.1.call-update
  344.7 0.0 all-gather.2.cloned.1.call-done
  344.8 5.2 convolution_convert_fusion
  350.0 1.3 copy.36
  351.2 0.8 multiply_add_fusion
  352.0 130.9 %all-reduce.8.cloned.1.call-done = f32[288,512]{1,0:T(8,128)} async-done(((f32[288,512]{1,0:T(8,128)}), f32[288,512]{1,0:T(8,128)}) %all-reduce.8.cloned.1.call-update) | async-done | bytes 589840 | tf_op jit(solution)/shard_map/psum | solution.py:55
  482.9 2.2 fusion.13
  485.1 1.1 convolution_bitcast_fusion.3
  486.3 70.8 %all-reduce.9 = bf16[288,512]{1,0:T(8,128)(2,1)S(1)} all-reduce(f32[288,512]{1,0:T(8,128)S(1)} %convolution_bitcast_fusion.3), channel_id=1, replica_groups=mesh['fsdp'=16,'factor'=16] {'factor'}, use_global_device_ids=true, to_apply=%region_4.5 | all-reduce | flops 147456 | bytes 884736 | tf_op jit(solution)/shard_map/psum | solution.py:67
  557.1 0.1 dynamic-slice_convert_fusion
  557.2 0.7 copy.34
  (25 shorter events, 0.1 us)
Async XLA Ops:
  8.0 474.9 %copy-start = (f32[512,512]{1,0:T(8,128)S(1)}, f32[512,512]{1,0:T(8,128)}, u32[]{:S(2)}) copy-start(f32[512,512]{1,0:T(8,128)} %param.13) | copy-start | bytes 3145732
  8.0 2.6 copy-start.1
  8.0 335.2 %all-reduce.6.cloned.1.call-start = ((), (), s32[]{:S(2)}) async-start(), calls=%async_computation.4 | async-start | bytes 2097152 | tf_op jit(solution)/shard_map/psum | solution.py:58
  10.5 2.0 copy-start.11
  10.5 334.2 %reduce-scatter.5.cloned.1.call-start = ((), (), s32[]{:S(2)}) async-start(), calls=%async_computation.5 | async-start | bytes 10027008 | tf_op jit(solution)/shard_map/reduce_scatter | solution.py:44
  11.1 1.4 copy-start.10
  20.1 73.2 %all-to-all-start = ((bf16[16,1,16,16,512]{4,3,2,1,0:T(8,128)(2,1)}), bf16[16,1,16,16,512]{4,3,2,1,0:T(8,128)(2,1)}, u32[]{:S(2)}, u32[]{:S(2)}) async-start(bf16[16,1,16,16,512]{4,3,2,1,0:T(8,128)(2,1)} %stack.2), calls=%async_computation | async-start | bytes 8388608 | tf_op jit(solution)/shard_map/all_to_all | solution.py:39
  25.5 319.2 %all-gather.2.cloned.1.call-start = ((), (), s32[]{:S(2)}) async-start(), calls=%async_computation.3 | async-start | bytes 5013504 | tf_op jit(solution)/shard_map/all_gather | solution.py:33
  26.1 323.9 %reduce-scatter.7.cloned.1.call-start = ((), (), s32[]{:S(2)}) async-start(), calls=%async_computation.7 | async-start | bytes 7520256
  115.4 4.7 copy-start.6
  120.1 3.7 copy-start.5
  123.8 3.7 copy-start.4
  129.8 4.7 copy-start.3
  134.6 3.8 copy-start.2
  172.9 170.3 %copy-start.9 = (f32[32,512]{1,0:T(8,128)S(1)}, f32[32,512]{1,0:T(8,128)}, u32[]{:S(2)}) copy-start(f32[32,512]{1,0:T(8,128)} %param.11) | copy-start | bytes 196612
  172.9 310.0 %all-reduce.8.cloned.1.call-start = ((), (), s32[]{:S(2)}) async-start(), calls=%async_computation.6 | async-start | bytes 1179648 | tf_op jit(solution)/shard_map/psum | solution.py:55
  344.8 6.5 %copy-start.8 = (f32[288,288]{1,0:T(8,128)S(1)}, f32[288,288]{1,0:T(8,128)}, u32[]{:S(2)}) copy-start(f32[288,288]{1,0:T(8,128)} %param.10) | copy-start | bytes 995332
  349.9 135.2 %copy-start.7 = (f32[288,288]{1,0:T(8,128)S(1)}, f32[288,288]{1,0:T(8,128)}, u32[]{:S(2)}) copy-start(f32[288,288]{1,0:T(8,128)} %param.12) | copy-start | bytes 995332
Sparse Core Ops, SparseCore 0:
  14.3 328.8 all-reduce.5
Sparse Core Ops, SparseCore 1:
  17.7 138.2 reduce-scatter.4
  157.7 76.9 all-gather.1
  237.3 89.6 reduce-scatter.6
  344.8 138.0 all-reduce.7
